TPU v7x, 32 devices: a whole 2x2x4 slice. The times are simulated.
32 devices in a mesh: parts: 2 (over y), src: 4 (over z), dst: 2 (over x), rep: 2 (over core).
Axes of the slice: x: 2, y: 2, z: 4, core: 2. Of those that a mesh axis runs over, the one named last changes fastest.
Arguments:
- edges: bfloat16 [8, 2, 2, 1024, 512], P(('parts', 'src'), 'dst', 'rep'), parts along dimension 0, may hold values from -6 to 6
- edge_count: int32 [8, 2, 2], P(('parts', 'src'), 'dst', 'rep'), parts along dimension 0, may hold values from 512 to 1024, as said below
- triplets: int32 [8, 2, 2, 3, 512], P(('parts', 'src'), 'dst', 'rep'), parts along dimension 0, may hold values from 0 to 63, as said below
- trip_count: int32 [8, 2, 2], P(('parts', 'src'), 'dst', 'rep'), parts along dimension 0, may hold values from 33 to 512, as said below
- rev_perm: int32 [8, 2, 2, 8], P(('parts', 'src'), 'dst', 'rep'), parts along dimension 0, may hold values from 0 to 7, each once within a row
- w_down: bfloat16 [512, 64], replicated, may hold values from -0.25 to 0.25
- w_up: bfloat16 [64, 512], replicated, may hold values from -0.25 to 0.25
- w_rev: bfloat16 [512, 512], replicated, may hold values from -0.25 to 0.25
- w_mlp1: bfloat16 [3, 512, 512], replicated, may hold values from -0.25 to 0.25
- w_mlp2: bfloat16 [3, 512, 512], replicated, may hold values from -0.25 to 0.25
- angular: bfloat16 [16, 128, 128], replicated, may hold values from -0.5 to 0.5
Outputs:
- updated: bfloat16 [8, 2, 2, 1024, 512], P(('parts', 'src'), 'dst', 'rep'), parts along dimension 0
There are 2 independent parts, one for each index of `parts`. A program takes and returns all parts, laid end to end along the dimension named above; an argument that names none is the same for every part. Nothing has to cross between parts.
Inputs may be any that keep to these rules, and one draw needn't show every extreme that they name: `edge_count`: some device has exactly 1024 live edges in every draw. `triplets`: row 0 holds reader blocks below 16, row 1 source blocks, row 2 bases below 16; slots at or beyond trip_count hold arbitrary values of the same ranges. `trip_count`: some device has exactly 512 live triplet blocks in every draw; loads differ strongly between devices.
All inputs are finite; a program needn't handle non-finite values.
Results may differ from a plain program's by a relative error of at most 0.0067.
Values may be sent and summed in bfloat16 or wider, within the bound.
A program may use at most 64 MiB of HBM per device.

v0:
```python
import jax
import jax.numpy as jnp
from jax import lax
from jax.sharding import PartitionSpec as P

GROUP = 64


root_three = 3.0 ** (-0.5)
root_two = 2.0 ** (-0.5)


def local(
    edges, edge_count, triplets, trip_count, rev_perm, w_down, w_up, w_rev, w_mlp1, w_mlp2, angular
):
    rows = edges.shape[3]
    width = edges.shape[4]
    blk = angular.shape[1]
    trip_width = w_down.shape[1]
    nblk = rows // blk
    slots = triplets.shape[4]
    own_rows = edges.reshape(rows, width)
    live = jnp.arange(rows, dtype=jnp.int32) < edge_count.reshape(())
    proj = jax.nn.silu(jnp.dot(own_rows, w_down, preferred_element_type=jnp.float32))
    proj = jnp.where(live[:, None], proj, jnp.float32(0.0)).astype(jnp.bfloat16)
    gathered = lax.all_gather(proj, ("src", "rep"), axis=0, tiled=True)
    blocks = gathered.reshape(-1, blk, trip_width)
    lists = triplets.reshape(3, slots)
    own_count = trip_count.reshape(())
    pair_size = lax.axis_size("rep")
    limit = lists.shape[1] - 1
    readers_all = jnp.arange(pair_size * nblk, dtype=jnp.int32)
    groups = (own_count + GROUP - 1) // GROUP

    def step(index, total_msg):
        position = index * GROUP + jnp.arange(GROUP, dtype=jnp.int32)
        valid = position < own_count
        picked = jnp.clip(position, 0, limit)
        entries = jnp.take(lists, picked, axis=1)
        source_blocks = blocks[entries[1]]
        matrices = angular[entries[2]]
        terms = jnp.einsum(
            "gij,gjc->gic", matrices, source_blocks, preferred_element_type=jnp.float32
        )
        terms = terms.reshape(GROUP, blk * trip_width)
        onehot = ((entries[0][None, :] == readers_all[:, None]) & valid[None, :]).astype(
            jnp.float32
        )
        return total_msg + jnp.dot(onehot, terms, precision=lax.Precision.HIGHEST)

    msg = lax.fori_loop(
        0, groups, step, jnp.zeros((pair_size * nblk, blk * trip_width), jnp.float32)
    )
    msg = lax.psum_scatter(msg, "rep", scatter_dimension=0, tiled=True)
    msg_b = msg.reshape(rows, trip_width).astype(jnp.bfloat16)
    trip = jax.nn.silu(jnp.dot(msg_b, w_up, preferred_element_type=jnp.float32))
    peers = lax.axis_size(("src", "dst"))
    pieces = own_rows.reshape(peers, rows // peers, width)
    spread = lax.all_to_all(pieces, ("src", "dst"), split_axis=0, concat_axis=0, tiled=True)
    spread = spread[::-1]
    partner = lax.all_to_all(
        spread, ("src", "dst"), split_axis=0, concat_axis=0, tiled=True
    ).reshape(rows, width)
    rev = partner.reshape(nblk, blk, width)[rev_perm.reshape(nblk)].reshape(rows, width)
    mixed = (
        own_rows.astype(jnp.float32)
        + trip
        + jnp.dot(rev, w_rev, preferred_element_type=jnp.float32)
    )
    state = (mixed * root_three).astype(jnp.bfloat16)
    for layer in range(w_mlp1.shape[0]):
        hidden = jax.nn.silu(
            jnp.dot(state, w_mlp1[layer], preferred_element_type=jnp.float32)
        ).astype(jnp.bfloat16)
        branch = jax.nn.silu(jnp.dot(hidden, w_mlp2[layer], preferred_element_type=jnp.float32))
        state = ((state.astype(jnp.float32) + branch) * root_two).astype(jnp.bfloat16)
    state = jnp.where(live[:, None], state, jnp.zeros_like(state))
    return state.reshape(1, 1, 1, rows, width)


def solution(mesh):
    in_specs = (
        P(("parts", "src"), "dst", "rep", None, None),
        P(("parts", "src"), "dst", "rep"),
        P(("parts", "src"), "dst", "rep", None, None),
        P(("parts", "src"), "dst", "rep"),
        P(("parts", "src"), "dst", "rep", None),
        P(),
        P(),
        P(),
        P(),
        P(),
        P(),
    )
    out_specs = P(("parts", "src"), "dst", "rep", None, None)
    return jax.shard_map(local, mesh=mesh, in_specs=in_specs, out_specs=out_specs, check_vma=False)
```

profile of v0, /device:TPU:8, one launch (start us, length us, event | category | flops | bytes accessed | tf_op | source)
XLA Modules:
  0.0 220.3 jit_solution(5634948870813638507)
XLA Ops:
  6.5 6.4 %all-to-all-start = ((bf16[8,128,512]{2,1,0:T(8,128)(2,1)}), bf16[8,128,512]{2,1,0:T(8,128)(2,1)S(1)}, u32[]{:S(2)}, u32[]{:S(2)}) async-start(bf16[8,128,512]{2,1,0:T(8,128)(2,1)} %bitcast.93), calls=%async_computation.1 | async-start | bytes 2097152 | tf_op jit(solution)/shard_map/all_to_all | solution.py:59
  15.6 28.7 %all-to-all-done = bf16[8,128,512]{2,1,0:T(8,128)(2,1)S(1)} async-done(((bf16[8,128,512]{2,1,0:T(8,128)(2,1)}), bf16[8,128,512]{2,1,0:T(8,128)(2,1)S(1)}, u32[]{:S(2)}, u32[]{:S(2)}) %all-to-all-start) | async-done | bytes 1048608 | tf_op jit(solution)/shard_map/all_to_all | solution.py:59
  45.4 7.0 %all-to-all-start.1 = ((bf16[8,128,512]{2,1,0:T(8,128)(2,1)}), bf16[8,128,512]{2,1,0:T(8,128)(2,1)}, u32[]{:S(2)}, u32[]{:S(2)}) async-start(bf16[8,128,512]{2,1,0:T(8,128)(2,1)} %rev.3), calls=%async_computation.2 | async-start | bytes 2097152 | tf_op jit(solution)/shard_map/all_to_all | solution.py:61
  56.1 133.8 %while.11 = (s32[]{:T(128)}, f32[16,8192]{1,0:T(8,128)}, s32[]{:T(128)}, s32[3,512]{0,1:T(8,128)S(1)}, s32[]{:T(128)}, /*index=5*/bf16[16,128,128]{2,1,0:T(8,128...) while((s32[]{:T(128)}, f32[16,8192]{1,0:T(8,128)}, s32[]{:T(128)}, ...), condition=%wide.region_1.2_spmd.clone, body=%wide.region_0.1_spmd.clone.sunk | while | flops 235018688 | bytes 18894708 | solution.py:51
  58.7 3.8 %gather_fusion.2 = bf16[64,128,64]{2,1,0:T(8,128)(2,1)} fusion(bf16[64,128,64]{2,1,0:T(8,128)(2,1)} %get-tuple-element.177, s32[1024]{0:T(1024)S(1)} %pad_clamp_fusion.9), kind=kCustom, calls=%fused_computation.2.clone.clone.1 | custom fusion | bytes 2097408 | tf_op jit(solution)/shard_map/while/body/gather | solution.py:40
  62.4 4.2 %fusion.79 = f32[64,128,64]{2,1,0:T(8,128)} fusion(bf16[64,128,128]{2,1,0:T(8,128)(2,1)S(1)} %gather_fusion.1, bf16[64,128,64]{2,1,0:T(8,128)(2,1)} %gather_fusion.2), kind=kOutput, calls=%fused_computation.63.clone.1 | convolution fusion | flops 134217728 | bytes 5242880 | tf_op jit(solution)/shard_map/while/body/gij,gjc->gic/dot_general | solution.py:42
  75.4 3.8 %gather_fusion.2 = bf16[64,128,64]{2,1,0:T(8,128)(2,1)} fusion(bf16[64,128,64]{2,1,0:T(8,128)(2,1)} %get-tuple-element.177, s32[1024]{0:T(1024)S(1)} %pad_clamp_fusion.9), kind=kCustom, calls=%fused_computation.2.clone.clone.1 | custom fusion | bytes 2097408 | tf_op jit(solution)/shard_map/while/body/gather | solution.py:40
  79.1 4.2 %fusion.79 = f32[64,128,64]{2,1,0:T(8,128)} fusion(bf16[64,128,128]{2,1,0:T(8,128)(2,1)S(1)} %gather_fusion.1, bf16[64,128,64]{2,1,0:T(8,128)(2,1)} %gather_fusion.2), kind=kOutput, calls=%fused_computation.63.clone.1 | convolution fusion | flops 134217728 | bytes 5242880 | tf_op jit(solution)/shard_map/while/body/gij,gjc->gic/dot_general | solution.py:42
  92.1 3.8 %gather_fusion.2 = bf16[64,128,64]{2,1,0:T(8,128)(2,1)} fusion(bf16[64,128,64]{2,1,0:T(8,128)(2,1)} %get-tuple-element.177, s32[1024]{0:T(1024)S(1)} %pad_clamp_fusion.9), kind=kCustom, calls=%fused_computation.2.clone.clone.1 | custom fusion | bytes 2097408 | tf_op jit(solution)/shard_map/while/body/gather | solution.py:40
  95.8 4.2 %fusion.79 = f32[64,128,64]{2,1,0:T(8,128)} fusion(bf16[64,128,128]{2,1,0:T(8,128)(2,1)S(1)} %gather_fusion.1, bf16[64,128,64]{2,1,0:T(8,128)(2,1)} %gather_fusion.2), kind=kOutput, calls=%fused_computation.63.clone.1 | convolution fusion | flops 134217728 | bytes 5242880 | tf_op jit(solution)/shard_map/while/body/gij,gjc->gic/dot_general | solution.py:42
  108.8 3.8 %gather_fusion.2 = bf16[64,128,64]{2,1,0:T(8,128)(2,1)} fusion(bf16[64,128,64]{2,1,0:T(8,128)(2,1)} %get-tuple-element.177, s32[1024]{0:T(1024)S(1)} %pad_clamp_fusion.9), kind=kCustom, calls=%fused_computation.2.clone.clone.1 | custom fusion | bytes 2097408 | tf_op jit(solution)/shard_map/while/body/gather | solution.py:40
  112.6 4.2 %fusion.79 = f32[64,128,64]{2,1,0:T(8,128)} fusion(bf16[64,128,128]{2,1,0:T(8,128)(2,1)S(1)} %gather_fusion.1, bf16[64,128,64]{2,1,0:T(8,128)(2,1)} %gather_fusion.2), kind=kOutput, calls=%fused_computation.63.clone.1 | convolution fusion | flops 134217728 | bytes 5242880 | tf_op jit(solution)/shard_map/while/body/gij,gjc->gic/dot_general | solution.py:42
  116.8 3.5 %reshape.213 = f32[64,8192]{1,0:T(8,128)S(1)} reshape(f32[64,128,64]{2,1,0:T(8,128)} %fusion.79) | data formatting | bytes 4194304 | tf_op jit(solution)/shard_map/while/body/reshape | solution.py:45
  125.5 3.8 %gather_fusion.2 = bf16[64,128,64]{2,1,0:T(8,128)(2,1)} fusion(bf16[64,128,64]{2,1,0:T(8,128)(2,1)} %get-tuple-element.177, s32[1024]{0:T(1024)S(1)} %pad_clamp_fusion.9), kind=kCustom, calls=%fused_computation.2.clone.clone.1 | custom fusion | bytes 2097408 | tf_op jit(solution)/shard_map/while/body/gather | solution.py:40
  129.3 4.2 %fusion.79 = f32[64,128,64]{2,1,0:T(8,128)} fusion(bf16[64,128,128]{2,1,0:T(8,128)(2,1)S(1)} %gather_fusion.1, bf16[64,128,64]{2,1,0:T(8,128)(2,1)} %gather_fusion.2), kind=kOutput, calls=%fused_computation.63.clone.1 | convolution fusion | flops 134217728 | bytes 5242880 | tf_op jit(solution)/shard_map/while/body/gij,gjc->gic/dot_general | solution.py:42
  142.2 3.8 %gather_fusion.2 = bf16[64,128,64]{2,1,0:T(8,128)(2,1)} fusion(bf16[64,128,64]{2,1,0:T(8,128)(2,1)} %get-tuple-element.177, s32[1024]{0:T(1024)S(1)} %pad_clamp_fusion.9), kind=kCustom, calls=%fused_computation.2.clone.clone.1 | custom fusion | bytes 2097408 | tf_op jit(solution)/shard_map/while/body/gather | solution.py:40
  146.0 4.2 %fusion.79 = f32[64,128,64]{2,1,0:T(8,128)} fusion(bf16[64,128,128]{2,1,0:T(8,128)(2,1)S(1)} %gather_fusion.1, bf16[64,128,64]{2,1,0:T(8,128)(2,1)} %gather_fusion.2), kind=kOutput, calls=%fused_computation.63.clone.1 | convolution fusion | flops 134217728 | bytes 5242880 | tf_op jit(solution)/shard_map/while/body/gij,gjc->gic/dot_general | solution.py:42
  159.0 3.8 %gather_fusion.2 = bf16[64,128,64]{2,1,0:T(8,128)(2,1)} fusion(bf16[64,128,64]{2,1,0:T(8,128)(2,1)} %get-tuple-element.177, s32[1024]{0:T(1024)S(1)} %pad_clamp_fusion.9), kind=kCustom, calls=%fused_computation.2.clone.clone.1 | custom fusion | bytes 2097408 | tf_op jit(solution)/shard_map/while/body/gather | solution.py:40
  162.7 4.2 %fusion.79 = f32[64,128,64]{2,1,0:T(8,128)} fusion(bf16[64,128,128]{2,1,0:T(8,128)(2,1)S(1)} %gather_fusion.1, bf16[64,128,64]{2,1,0:T(8,128)(2,1)} %gather_fusion.2), kind=kOutput, calls=%fused_computation.63.clone.1 | convolution fusion | flops 134217728 | bytes 5242880 | tf_op jit(solution)/shard_map/while/body/gij,gjc->gic/dot_general | solution.py:42
  175.7 3.8 %gather_fusion.2 = bf16[64,128,64]{2,1,0:T(8,128)(2,1)} fusion(bf16[64,128,64]{2,1,0:T(8,128)(2,1)} %get-tuple-element.177, s32[1024]{0:T(1024)S(1)} %pad_clamp_fusion.9), kind=kCustom, calls=%fused_computation.2.clone.clone.1 | custom fusion | bytes 2097408 | tf_op jit(solution)/shard_map/while/body/gather | solution.py:40
  179.4 4.2 %fusion.79 = f32[64,128,64]{2,1,0:T(8,128)} fusion(bf16[64,128,128]{2,1,0:T(8,128)(2,1)S(1)} %gather_fusion.1, bf16[64,128,64]{2,1,0:T(8,128)(2,1)} %gather_fusion.2), kind=kOutput, calls=%fused_computation.63.clone.1 | convolution fusion | flops 134217728 | bytes 5242880 | tf_op jit(solution)/shard_map/while/body/gij,gjc->gic/dot_general | solution.py:42
  189.9 6.8 %reduce-scatter.2.cloned.1.call-done = f32[8,8192]{1,0:T(8,128)} async-done(((f32[16,8192]{1,0:T(8,128)}), f32[8,8192]{1,0:T(8,128)}) %reduce-scatter.2.cloned.1.call-update) | async-done | bytes 262160 | tf_op jit(solution)/shard_map/reduce_scatter | solution.py:54
  202.4 3.8 %multiply_convert_fusion.4 = bf16[1024,512]{1,0:T(8,128)(2,1)} fusion(bf16[1024,512]{1,0:T(8,128)(2,1)S(1)} %multiply_convert_fusion.6, bf16[3,512,512]{2,1,0:T(8,128)(2,1)S(1)} %copy-done.5, bf16[3,512,512]{2,1,0:T(8,128)(2,1)} %param.21), kind=kOutput, calls=%fused_computation.31 | convolution fusion | flops 1080557568 | bytes 4194304 | tf_op jit(solution)/shard_map/dot_general | solution.py:75
  209.6 3.8 %select_bitcast_fusion.1 = bf16[1,1,1,1024,512]{4,3,2,1,0:T(8,128)(2,1)} fusion(pred[1024]{0:T(1024)(128)(4,1)S(1)} %iota_compare_fusion.1, bf16[1024,512]{1,0:T(8,128)(2,1)S(1)} %multiply_convert_fusion.2, bf16[3,512,512]{2,1,0:T(8,128)(2,1)S(1)} %copy-done.5, bf16[3,512,512]{2,1,0:T(8,128)(2,1)} %param.21), kind=kOutput, calls=%fused_computation.36 | convolution fusion | flops 1081081856 | bytes 4195328 | tf_op jit(solution)/shard_map/dot_general | solution.py:75
  (141 shorter events, 80.9 us)
Async XLA Ops:
  6.5 193.3 %copy-start = (bf16[512,512]{1,0:T(8,128)(2,1)S(1)}, bf16[512,512]{1,0:T(8,128)(2,1)}, u32[]{:S(2)}) copy-start(bf16[512,512]{1,0:T(8,128)(2,1)} %param.20) | copy-start | bytes 1572868
  6.5 7.1 %copy-start.2 = (bf16[1,1,1,1024,512]{4,3,2,1,0:T(8,128)(2,1)S(1)}, bf16[1,1,1,1024,512]{4,3,2,1,0:T(8,128)(2,1)}, u32[]{:S(2)}) copy-start(bf16[1,1,1,1024,512]{4,3,2,1,0:T(8,128)(2,1)} %param.13) | copy-start | bytes 3145732
  6.5 7.1 %copy-start.6 = (bf16[512,64]{0,1:T(8,128)(2,1)S(1)}, bf16[512,64]{0,1:T(8,128)(2,1)}, u32[]{:S(2)}) copy-start(bf16[512,64]{0,1:T(8,128)(2,1)} %param.18) | copy-start | bytes 196612
  6.5 8.9 %copy-start.4 = (s32[1,1,1,3,512]{4,2,3,1,0:T(1,128)S(1)}, s32[1,1,1,3,512]{4,2,3,1,0:T(1,128)}, u32[]{:S(2)}) copy-start(s32[1,1,1,3,512]{4,2,3,1,0:T(1,128)} %param.15) | copy-start | bytes 18436
  6.5 37.7 %all-to-all-start = ((bf16[8,128,512]{2,1,0:T(8,128)(2,1)}), bf16[8,128,512]{2,1,0:T(8,128)(2,1)S(1)}, u32[]{:S(2)}, u32[]{:S(2)}) async-start(bf16[8,128,512]{2,1,0:T(8,128)(2,1)} %bitcast.93), calls=%async_computation.1 | async-start | bytes 2097152 | tf_op jit(solution)/shard_map/all_to_all | solution.py:59
  12.9 39.5 %all-gather.2.cloned.1.call-start = ((), (), s32[]{:S(2)}) async-start(), calls=%async_computation.3 | async-start | bytes 1179648 | tf_op jit(solution)/shard_map/all_gather | solution.py:26
  45.4 152.6 %all-to-all-start.1 = ((bf16[8,128,512]{2,1,0:T(8,128)(2,1)}), bf16[8,128,512]{2,1,0:T(8,128)(2,1)}, u32[]{:S(2)}, u32[]{:S(2)}) async-start(bf16[8,128,512]{2,1,0:T(8,128)(2,1)} %rev.3), calls=%async_computation.2 | async-start | bytes 2097152 | tf_op jit(solution)/shard_map/all_to_all | solution.py:61
  52.4 3.7 %copy-start.1 = (bf16[16,128,128]{2,1,0:T(8,128)(2,1)S(1)}, bf16[16,128,128]{2,1,0:T(8,128)(2,1)}, u32[]{:S(2)}) copy-start(bf16[16,128,128]{2,1,0:T(8,128)(2,1)} %param.23) | copy-start | bytes 1572868
  52.4 144.3 %reduce-scatter.2.cloned.1.call-start = ((), (), s32[]{:S(2)}) async-start(), calls=%async_computation.4 | async-start | bytes 786432 | tf_op jit(solution)/shard_map/reduce_scatter | solution.py:54
  56.1 133.8 %copy-start.8 = (s32[1,1,1,8]{3,2,1,0:T(1,128)S(1)}, s32[1,1,1,8]{3,2,1,0:T(1,128)}, u32[]{:S(2)}) copy-start(s32[1,1,1,8]{3,2,1,0:T(1,128)} %param.17) | copy-start | bytes 100
  199.8 1.2 copy-start.3
  199.8 1.2 copy-start.7
  201.0 1.4 copy-start.5
Sparse Core Ops, SparseCore 0:
  15.4 31.9 all-gather.1
  190.0 6.6 reduce-scatter.1
where the time goes:
time: 224 us; the launch traced here: 220 us
  local copies, waits for them, and re-layouts  80 us (36%)
  matrix products  68.7 us (31%)
  waiting for transfers between devices  35.5 us (16%)
  between operations  14.9 us (7%)
  starting transfers between devices  13.4 us (6%)
  other arithmetic  7.13 us (3%)
    dot_general x8, matrix products, step(): jnp.einsum('gij,gjc->gic', matrices, source_blocks, preferred_element_typ...  33.9 us
    gather x8, local copies, waits for them, and re-layouts, step(): source_blocks = blocks[entries[1]]  30 us
    all_to_all x1, waiting for transfers between devices, local(): lax.all_to_all(pieces, ('src', 'dst'), split_axis=0, concat_axis=0, tiled...  28.7 us
    reshape x8, local copies, waits for them, and re-layouts, step(): terms = terms.reshape(GROUP, blk * trip_width)  28.1 us
    dot_general x8, matrix products, step(): return total_msg + jnp.dot(onehot, terms, precision=lax.Precision.HIGHEST)  21.1 us
    dot_general x3, matrix products, local(): jnp.dot(hidden, w_mlp2[layer], preferred_element_type=jnp.float32)  11 us
    gather x8, local copies, waits for them, and re-layouts, step(): matrices = angular[entries[2]]  7.61 us
    all_to_all x1, starting transfers between devices, local(): lax.all_to_all(spread, ('src', 'dst'), split_axis=0, concat_axis=0, tiled...  7.04 us
  transfers between devices with their start and end apart: 4, of which 2 were waited for; matrix products, arithmetic and copies ran while one was open for 64% of the time, Pallas kernels for 0%

commit v1 on v0

v1 whole, which is shorter than its diff:
```python
import jax
import jax.numpy as jnp
from jax import lax
from jax.sharding import PartitionSpec as P

root_three = 3.0 ** (-0.5)
root_two = 2.0 ** (-0.5)


def local(
    edges, edge_count, triplets, trip_count, rev_perm, w_down, w_up, w_rev, w_mlp1, w_mlp2, angular
):
    rows = edges.shape[3]
    width = edges.shape[4]
    blk = angular.shape[1]
    bases = angular.shape[0]
    trip_width = w_down.shape[1]
    nblk = rows // blk
    slots = triplets.shape[4]
    own_rows = edges.reshape(rows, width)
    n_src, n_dst = lax.axis_size("src"), lax.axis_size("dst")
    peers = n_src * n_dst
    mirror = [(q, peers - 1 - q) for q in range(peers)]
    partner = lax.ppermute(own_rows, ("src", "dst"), mirror)
    live = jnp.arange(rows, dtype=jnp.int32) < edge_count.reshape(())
    proj = jax.nn.silu(jnp.dot(own_rows, w_down, preferred_element_type=jnp.float32))
    proj = jnp.where(live[:, None], proj, jnp.float32(0.0)).astype(jnp.bfloat16)
    gathered = lax.all_gather(proj, ("src", "rep"), axis=0, tiled=True)
    blocks = gathered.reshape(-1, blk, trip_width)
    lists = triplets.reshape(3, slots)
    pair_size = lax.axis_size("rep")
    readers = pair_size * nblk
    valid = jnp.arange(slots, dtype=jnp.int32) < trip_count.reshape(())
    code = jnp.where(valid, lists[0] * bases + lists[2], -1)
    hot_code = (code[None, :] == jnp.arange(readers * bases, dtype=jnp.int32)[:, None]).astype(jnp.bfloat16)
    hot_source = (lists[1][None, :] == jnp.arange(blocks.shape[0], dtype=jnp.int32)[:, None]).astype(jnp.bfloat16)
    counts = lax.dot_general(hot_code, hot_source, (((1,), (1,)), ((), ())), preferred_element_type=jnp.float32)
    upper = jnp.floor(counts * (1.0 / 256.0)) * 256.0
    both = jnp.stack([(counts - upper), upper]).astype(jnp.bfloat16)
    sums = jnp.einsum("pxc,cjh->xjh", both, blocks, preferred_element_type=jnp.float32)
    sums = sums.reshape(readers, bases, blk, trip_width)
    high = sums.astype(jnp.bfloat16)
    low = (sums - high.astype(jnp.float32)).astype(jnp.bfloat16)
    msg = jnp.einsum("kij,pakjh->aih", angular, jnp.stack([high, low]), preferred_element_type=jnp.float32)
    msg = lax.psum_scatter(msg.reshape(readers, blk * trip_width), "rep", scatter_dimension=0, tiled=True)
    msg_b = msg.reshape(rows, trip_width).astype(jnp.bfloat16)
    trip = jax.nn.silu(jnp.dot(msg_b, w_up, preferred_element_type=jnp.float32))
    rev = partner.reshape(nblk, blk, width)[rev_perm.reshape(nblk)].reshape(rows, width)
    mixed = (
        own_rows.astype(jnp.float32)
        + trip
        + jnp.dot(rev, w_rev, preferred_element_type=jnp.float32)
    )
    state = (mixed * root_three).astype(jnp.bfloat16)
    for layer in range(w_mlp1.shape[0]):
        hidden = jax.nn.silu(
            jnp.dot(state, w_mlp1[layer], preferred_element_type=jnp.float32)
        ).astype(jnp.bfloat16)
        branch = jax.nn.silu(jnp.dot(hidden, w_mlp2[layer], preferred_element_type=jnp.float32))
        state = ((state.astype(jnp.float32) + branch) * root_two).astype(jnp.bfloat16)
    state = jnp.where(live[:, None], state, jnp.zeros_like(state))
    return state.reshape(1, 1, 1, rows, width)


def solution(mesh):
    in_specs = (
        P(("parts", "src"), "dst", "rep", None, None),
        P(("parts", "src"), "dst", "rep"),
        P(("parts", "src"), "dst", "rep", None, None),
        P(("parts", "src"), "dst", "rep"),
        P(("parts", "src"), "dst", "rep", None),
        P(),
        P(),
        P(),
        P(),
        P(),
        P(),
    )
    out_specs = P(("parts", "src"), "dst", "rep", None, None)
    return jax.shard_map(local, mesh=mesh, in_specs=in_specs, out_specs=out_specs, check_vma=False)
```

time: 224 us -> 102 us (0.46); the launches traced: 220 us -> 101 us
  local copies, waits for them, and re-layouts: 80 us -> 4.77 us
  matrix products: 68.7 us -> 23.6 us
  waiting for transfers between devices: 35.5 us -> 46.6 us
  starting transfers between devices: 13.4 us -> 2.61 us
    dot_general x16 -> x3, matrix products: 55 us -> 6.98 us  [the longest x1 3.55 us: local(): jnp.einsum('kij,pakjh->aih', angular, jnp.stack([high, low]), preferred_e...]
    gather x24 -> x0, local copies, waits for them, and re-layouts: 42.4 us -> none  [the longest x8 30 us: step(): source_blocks = blocks[entries[1]]]
    all_gather x1, waiting for transfers between devices: 0.01 us -> 39.1 us  [local(): gathered = lax.all_gather(proj, ('src', 'rep'), axis=0, tiled=True)]
    all_to_all x2 -> x0, waiting for transfers between devices: 28.7 us -> none  [the longest x1 28.7 us: local(): lax.all_to_all(pieces, ('src', 'dst'), split_axis=0, concat_axis=0, tiled...]
    reshape x8 -> x1, local copies, waits for them, and re-layouts: 28.1 us -> 1.15 us  [local(): msg.reshape(readers, blk * trip_width)]
    all_to_all x2 -> x0, starting transfers between devices: 13.4 us -> none  [the longest x1 7.04 us: local(): lax.all_to_all(spread, ('src', 'dst'), split_axis=0, concat_axis=0, tiled...]
    reduce_sum x0 -> x2, other arithmetic: none -> 7.06 us  [the longest x1 7.05 us: local(): jnp.einsum('kij,pakjh->aih', angular, jnp.stack([high, low]), preferred_e...]
    and x8 -> x0, other arithmetic: 5.25 us -> none  [step(): entries = jnp.take(lists, picked, axis=1)]
  transfers between devices with their start and end apart: 4 -> 3, of which waited for: 2 -> 2; matrix products, arithmetic and copies ran while one was open for 64% -> 18% of each run, Pallas kernels for 0% -> 0%
where the time goes in v1:
time: 102 us; the launch traced here: 101 us
  waiting for transfers between devices  46.6 us (46%)
  matrix products  23.6 us (23%)
  between operations  14.9 us (15%)
  other arithmetic  8.05 us (8%)
  local copies, waits for them, and re-layouts  4.77 us (5%)
  starting transfers between devices  2.61 us (3%)
    all_gather x1, waiting for transfers between devices, local(): gathered = lax.all_gather(proj, ('src', 'rep'), axis=0, tiled=True)  39.1 us
    dot_general x3, matrix products, local(): jnp.dot(hidden, w_mlp2[layer], preferred_element_type=jnp.float32)  11.8 us
    reduce_scatter x1, waiting for transfers between devices, local(): lax.psum_scatter(msg.reshape(readers, blk * trip_width), 'rep', scatter_d...  7.46 us
    reduce_sum x1, other arithmetic, local(): jnp.einsum('kij,pakjh->aih', angular, jnp.stack([high, low]), preferred_e...  7.05 us
    dot_general x1, matrix products, local(): jnp.einsum('kij,pakjh->aih', angular, jnp.stack([high, low]), preferred_e...  3.55 us
    dot_general x1, matrix products, local(): jnp.einsum('pxc,cjh->xjh', both, blocks, preferred_element_type=jnp.float32)  3.19 us
    ppermute x1, starting transfers between devices, local(): partner = lax.ppermute(own_rows, ('src', 'dst'), mirror)  2.57 us
    dot_general x1, matrix products, local(): jnp.dot(own_rows, w_down, preferred_element_type=jnp.float32)  2.36 us
  transfers between devices with their start and end apart: 3, of which 2 were waited for; matrix products, arithmetic and copies ran while one was open for 18% of the time, Pallas kernels for 0%

profile of v1, /device:TPU:8, one launch (start us, length us, event | category | flops | bytes accessed | tf_op | source)
XLA Modules:
  0.0 100.6 jit_solution(11920454833546234623)
XLA Ops:
  7.3 2.4 %select_convert_fusion = bf16[1024,64]{0,1:T(8,128)(2,1)} fusion(pred[1024]{0:T(1024)(128)(4,1)S(1)} %iota_compare_fusion.4, bf16[512,64]{0,1:T(8,128)(2,1)} %param.16, bf16[1,1,1,1024,512]{4,3,2,1,0:T(8,128)(2,1)} %param.11), kind=kOutput, calls=%fused_computation.37 | convolution fusion | flops 67502080 | bytes 1246208 | tf_op jit(solution)/shard_map/dot_general | solution.py:26
  9.6 0.0 all-gather.2.cloned.1.call-update
  9.7 0.0 reduce-scatter.2.cloned.1.call-start
  9.7 2.6 %collective-permute-start = (bf16[1024,512]{1,0:T(8,128)(2,1)}, bf16[1024,512]{1,0:T(8,128)(2,1)S(1)}, u32[]{:S(2)}, u32[]{:S(2)}) collective-permute-start(bf16[1024,512]{1,0:T(8,128)(2,1)} %bitcast.93), channel_id=1, source_target_pairs={{0,14},{2,12},{4,10},{6,8},{8,6},{10,4},{12,2},{14,0},{1,15},{3,13... | collective-permute-start | bytes 3145736 | tf_op jit(solution)/shard_map/ppermute | solution.py:24
  13.0 0.2 fusion.45
  13.2 0.1 copy.16
  13.3 39.1 %all-gather.2.cloned.1.call-done = bf16[8192,64]{0,1:T(8,128)(2,1)} async-done(((bf16[1024,64]{0,1:T(8,128)(2,1)}), bf16[8192,64]{0,1:T(8,128)(2,1)}) %all-gather.2.cloned.1.call-update) | async-done | bytes 1048592 | tf_op jit(solution)/shard_map/all_gather | solution.py:28
  52.4 1.5 %copy.21 = bf16[8,8,64,128]{3,2,1,0:T(8,128)(2,1)S(1)} copy(bf16[8,8,64,128]{3,1,2,0:T(8,128)(2,1)} %bitcast.89) | data formatting | bytes 2097152
  53.9 3.2 %convert_bitcast_fusion = (bf16[1,16,16,128,64]{3,2,4,1,0:T(8,128)(2,1)S(1)}, bf16[1,16,16,128,64]{3,2,4,1,0:T(8,128)(2,1)}) fusion(bf16[16,16,64,1]{2,1,3,0:T(8,128)(2,1)S(1)} %bitcast.90, bf16[64,128,64,1]{1,0,2,3:T(8,128)(2,1)S(1)} %bitcast.86), kind=kOutput, calls=%fused_computation.13 | convolution fusion | flops 276824064 | bytes 9469952 | tf_op jit(solution)/shard_map/pxc,cjh->xjh/dot_general | solution.py:40
  57.1 7.1 %convert_reduce_fusion = bf16[16,16,128,64]{2,1,3,0:T(8,128)(2,1)} fusion(bf16[1,16,16,128,64]{3,2,4,1,0:T(8,128)(2,1)} %get-tuple-element.6, bf16[1,16,16,128,64]{3,2,4,1,0:T(8,128)(2,1)S(1)} %get-tuple-element.5), kind=kLoop, calls=%fused_computation.1 | loop fusion | flops 18874368 | bytes 12582912 | tf_op jit(solution)/shard_map/kij,pakjh->aih/reduce_sum | solution.py:44
  64.2 3.6 %fusion.3 = f32[16,128,64]{1,2,0:T(8,128)S(1)} fusion(bf16[16,16,128,64]{2,1,3,0:T(8,128)(2,1)} %convert_reduce_fusion, bf16[16,128,128]{2,1,0:T(8,128)(2,1)} %param.21), kind=kOutput, calls=%fused_computation.14 | convolution fusion | flops 536870912 | bytes 5242880 | tf_op jit(solution)/shard_map/kij,pakjh->aih/dot_general | solution.py:44
  67.8 0.3 copy.18
  68.1 1.2 %reshape.92 = f32[16,8192]{1,0:T(8,128)} reshape(f32[16,128,64]{2,1,0:T(8,128)S(1)} %copy.18) | data formatting | bytes 1048576 | tf_op jit(solution)/shard_map/reshape | solution.py:45
  69.3 0.0 reduce-scatter.2.cloned.1.call-update
  69.3 0.6 gather_fusion
  69.9 7.5 %reduce-scatter.2.cloned.1.call-done = f32[8,8192]{1,0:T(8,128)} async-done(((f32[16,8192]{1,0:T(8,128)}), f32[8,8192]{1,0:T(8,128)}) %reduce-scatter.2.cloned.1.call-update) | async-done | bytes 262160 | tf_op jit(solution)/shard_map/reduce_scatter | solution.py:45
  77.4 1.0 convert_element_type.67
  78.4 0.2 convert_element_type.68
  78.6 0.4 fusion.56
  79.1 0.8 copy-done.4
  79.9 2.1 %multiply_convert_fusion.6 = bf16[1024,512]{1,0:T(8,128)(2,1)} fusion(f32[1024,512]{1,0:T(8,128)S(1)} %fusion.56, bf16[1024,512]{1,0:T(8,128)(2,1)S(1)} %bitcast.88, bf16[512,512]{1,0:T(8,128)(2,1)S(1)} %copy-done, bf16[1,1,1,1024,512]{4,3,2,1,0:T(8,128)(2,1)S(1)} %copy-done.4), kind=kOutput, calls=%fused_computation.12 | convolution fusion | flops 541589504 | bytes 5767168 | tf_op jit(solution)/shard_map/dot_general | solution.py:52
  81.9 4.5 %multiply_convert_fusion.4 = bf16[1024,512]{1,0:T(8,128)(2,1)} fusion(bf16[1024,512]{1,0:T(8,128)(2,1)} %multiply_convert_fusion.6, bf16[3,512,512]{2,1,0:T(8,128)(2,1)S(1)} %copy-done.3, bf16[3,512,512]{2,1,0:T(8,128)(2,1)} %param.19), kind=kOutput, calls=%fused_computation.10 | convolution fusion | flops 1080557568 | bytes 4194304 | tf_op jit(solution)/shard_map/dot_general | solution.py:59
  86.4 3.5 %multiply_convert_fusion.2 = bf16[1024,512]{1,0:T(8,128)(2,1)S(1)} fusion(bf16[1024,512]{1,0:T(8,128)(2,1)} %multiply_convert_fusion.4, bf16[3,512,512]{2,1,0:T(8,128)(2,1)S(1)} %copy-done.3, bf16[3,512,512]{2,1,0:T(8,128)(2,1)} %param.19), kind=kOutput, calls=%fused_computation.8 | convolution fusion | flops 1080557568 | bytes 4194304 | tf_op jit(solution)/shard_map/dot_general | solution.py:59
  89.9 3.8 %select_bitcast_fusion = bf16[1,1,1,1024,512]{4,3,2,1,0:T(8,128)(2,1)} fusion(pred[1024]{0:T(1024)(128)(4,1)S(1)} %iota_compare_fusion.4, bf16[1024,512]{1,0:T(8,128)(2,1)S(1)} %multiply_convert_fusion.2, bf16[3,512,512]{2,1,0:T(8,128)(2,1)S(1)} %copy-done.3, bf16[3,512,512]{2,1,0:T(8,128)(2,1)} %param.19), kind=kOutput, calls=%fused_computation.15 | convolution fusion | flops 1081081856 | bytes 4195328 | tf_op jit(solution)/shard_map/dot_general | solution.py:59
  (19 shorter events, 0.1 us)
Async XLA Ops:
  6.5 72.5 %copy-start = (bf16[512,512]{1,0:T(8,128)(2,1)S(1)}, bf16[512,512]{1,0:T(8,128)(2,1)}, u32[]{:S(2)}) copy-start(bf16[512,512]{1,0:T(8,128)(2,1)} %param.18) | copy-start | bytes 1572868
  6.5 6.4 %copy-start.2 = (s32[1,1,1,3,512]{4,2,3,1,0:T(1,128)S(1)}, s32[1,1,1,3,512]{4,2,3,1,0:T(1,128)}, u32[]{:S(2)}) copy-start(s32[1,1,1,3,512]{4,2,3,1,0:T(1,128)} %param.13) | copy-start | bytes 18436
  6.5 45.9 %all-gather.2.cloned.1.call-start = ((), (), s32[]{:S(2)}) async-start(), calls=%async_computation.1 | async-start | bytes 1179648 | tf_op jit(solution)/shard_map/all_gather | solution.py:28
  9.7 67.8 %reduce-scatter.2.cloned.1.call-start = ((), (), s32[]{:S(2)}) async-start(), calls=%async_computation.2 | async-start | bytes 786432 | tf_op jit(solution)/shard_map/reduce_scatter | solution.py:45
  9.7 59.6 %collective-permute-start = (bf16[1024,512]{1,0:T(8,128)(2,1)}, bf16[1024,512]{1,0:T(8,128)(2,1)S(1)}, u32[]{:S(2)}, u32[]{:S(2)}) collective-permute-start(bf16[1024,512]{1,0:T(8,128)(2,1)} %bitcast.93), channel_id=1, source_target_pairs={{0,14},{2,12},{4,10},{6,8},{8,6},{10,4},{12,2},{14,0},{1,15},{3,13... | collective-permute-start | bytes 3145736 | tf_op jit(solution)/shard_map/ppermute | solution.py:24
  67.7 1.5 %copy-start.5 = (s32[1,1,1,8]{3,2,1,0:T(1,128)S(1)}, s32[1,1,1,8]{3,2,1,0:T(1,128)}, u32[]{:S(2)}) copy-start(s32[1,1,1,8]{3,2,1,0:T(1,128)} %param.15) | copy-start | bytes 100
  69.3 9.4 %copy-start.1 = (bf16[64,512]{1,0:T(8,128)(2,1)S(1)}, bf16[64,512]{1,0:T(8,128)(2,1)}, u32[]{:S(2)}) copy-start(bf16[64,512]{1,0:T(8,128)(2,1)} %param.17) | copy-start | bytes 196612
  78.6 1.2 %copy-start.4 = (bf16[1,1,1,1024,512]{4,3,2,1,0:T(8,128)(2,1)S(1)}, bf16[1,1,1,1024,512]{4,3,2,1,0:T(8,128)(2,1)}, u32[]{:S(2)}) copy-start(bf16[1,1,1,1024,512]{4,3,2,1,0:T(8,128)(2,1)} %param.11) | copy-start | bytes 3145732
  79.9 2.1 %copy-start.3 = (bf16[3,512,512]{2,1,0:T(8,128)(2,1)S(1)}, bf16[3,512,512]{2,1,0:T(8,128)(2,1)}, u32[]{:S(2)}) copy-start(bf16[3,512,512]{2,1,0:T(8,128)(2,1)} %param.20) | copy-start | bytes 4718596
Sparse Core Ops, SparseCore 0:
  9.8 42.6 all-gather.1
  69.4 7.9 reduce-scatter.1

commit v2 on v1

v2 whole, which is shorter than its diff:
```python
import functools

import jax
import jax.numpy as jnp
from jax import lax
from jax.experimental import pallas as pl
from jax.experimental.pallas import tpu as pltpu
from jax.sharding import PartitionSpec as P

root_three = 3.0 ** (-0.5)
root_two = 2.0 ** (-0.5)
MESH = pl.DeviceIdType.MESH
HEAD = 3


def silu(v):
    return v * (0.5 + 0.5 * jnp.tanh(v * 0.5))


def mixed_dot(a, b, da, db):
    return lax.dot_general(a, b, (((da,), (db,)), ((), ())), preferred_element_type=jnp.float32)


def kernel(
    sizes, edge_count, trip_count, perm, lists, w_down, w_up, edges_in, rev_in, mlp1_in, mlp2_in, ang_in, out,
    edges, rev, w_rev, mlp1, mlp2, ang, acat, proj, gath, high, low, msg, part, give, take, pre, done,
    load_sem, bulk_send, bulk_recv, right_send, left_send, pair_send, gath_recv, msg_send, msg_recv,
):
    n_src, n_dst, n_rep = sizes
    s, d, r = lax.axis_index("src"), lax.axis_index("dst"), lax.axis_index("rep")
    rows, width = edges.shape
    bases, blk = ang.shape[0], ang.shape[1]
    nblk = rows // blk
    shift = nblk.bit_length() - 1
    trip_width = w_down.shape[1]
    slots = lists.shape[1]
    readers = n_rep * nblk
    codes = readers * bases
    mirror = {"src": n_src - 1 - s, "dst": n_dst - 1 - d}
    pair = {"rep": 1 - r}
    right = {"src": jnp.minimum(s + 1, n_src - 1)}
    left = {"src": jnp.maximum(s - 1, 0)}
    has_right, has_left = s + 1 < n_src, s > 0

    loads = [
        pltpu.make_async_copy(source, target, load_sem.at[index])
        for index, (source, target) in enumerate(
            [(edges_in, edges), (ang_in, ang), (rev_in, w_rev), (mlp1_in, mlp1), (mlp2_in, mlp2)]
        )
    ]
    for load in loads:
        load.start()

    barrier = pltpu.get_barrier_semaphore()
    pl.semaphore_signal(barrier, inc=1, device_id=mirror, device_id_type=MESH)
    pl.semaphore_signal(barrier, inc=1, device_id=pair, device_id_type=MESH)

    @pl.when(has_right)
    def _():
        pl.semaphore_signal(barrier, inc=1, device_id=right, device_id_type=MESH)

    @pl.when(has_left)
    def _():
        pl.semaphore_signal(barrier, inc=1, device_id=left, device_id_type=MESH)

    pl.semaphore_wait(barrier, 2 + has_right.astype(jnp.int32) + has_left.astype(jnp.int32))

    def bulk(m):
        span = pl.ds(pl.multiple_of(m * blk, blk), blk)
        return pltpu.make_async_remote_copy(
            src_ref=edges_in.at[span], dst_ref=rev.at[span],
            send_sem=bulk_send.at[m], recv_sem=bulk_recv.at[m], device_id=mirror, device_id_type=MESH,
        )

    def chunk(q, sems, o, target):
        return pltpu.make_async_remote_copy(
            src_ref=gath.at[q], dst_ref=gath.at[q],
            send_sem=sems.at[o], recv_sem=gath_recv.at[q], device_id=target, device_id_type=MESH,
        )

    for m in range(HEAD):
        bulk(m).start()

    loads[0].wait()
    lane = lax.broadcasted_iota(jnp.int32, (trip_width, blk), 1)
    down = w_down[...]
    for b in range(nblk):
        value = silu(mixed_dot(down, edges[b * blk:(b + 1) * blk, :], 0, 1))
        value = jnp.where(lane + b * blk < edge_count[0], value, 0.0)
        proj[pl.ds(b, trip_width, stride=nblk), :] = value
    own = s * n_rep + r
    gath[own] = proj[...].astype(jnp.bfloat16)
    chunk(own, pair_send, s, pair).start()

    @pl.when(has_right)
    def _():
        chunk(own, right_send, s, right).start()

    @pl.when(has_left)
    def _():
        chunk(own, left_send, s, left).start()

    for m in range(HEAD, nblk):
        bulk(m).start()

    loads[1].wait()
    for k in range(bases):
        acat[:, k * blk:(k + 1) * blk] = ang[k]
    a, c, k = lists[0:1, :], lists[1:2, :], lists[2:3, :]
    slot = lax.broadcasted_iota(jnp.int32, (1, slots), 1)
    code = jnp.where(slot < trip_count[0], k * readers + a, -1)
    hot_code = jnp.where(lax.broadcasted_iota(jnp.int32, (codes, slots), 0) == code, 1.0, 0.0).astype(jnp.bfloat16)
    cols = n_src * n_rep * nblk * 2
    line = lax.broadcasted_iota(jnp.int32, (cols, slots), 0)
    line = ((line >> (shift + 1)) << shift) + (line & (nblk - 1))
    hot_source = jnp.where(line == c, 1.0, 0.0).astype(jnp.bfloat16)
    counts = mixed_dot(hot_code, hot_source, 1, 1)
    odd = (lax.broadcasted_iota(jnp.int32, (codes, cols), 1) >> shift) & 1
    counts = jnp.concatenate([jnp.where(odd == 0, counts, 0.0), jnp.where(odd == 1, counts, 0.0)], axis=0)
    upper = jnp.floor(counts * (1.0 / 256.0)) * 256.0
    lower = (counts - upper).astype(jnp.bfloat16)
    upper = upper.astype(jnp.bfloat16)

    for hop in range(1, n_src):
        before, after = s - hop, s + hop

        @pl.when(before >= 0)
        def _():
            o = jnp.maximum(before, 0)
            q = o * n_rep + r
            chunk(q, left_send, o, left).wait_recv()

            @pl.when(has_right)
            def _():
                chunk(q, right_send, o, right).start()

            chunk(q, pair_send, o, pair).start()

        @pl.when(after < n_src)
        def _():
            o = jnp.minimum(after, n_src - 1)
            q = o * n_rep + r
            chunk(q, right_send, o, right).wait_recv()

            @pl.when(has_left)
            def _():
                chunk(q, left_send, o, left).start()

            chunk(q, pair_send, o, pair).start()

    for o in range(n_src):
        chunk(o * n_rep + 1 - r, pair_send, o, pair).wait_recv()

    def project(p, carry):
        halves = [
            gath[:, pl.ds(pl.multiple_of((2 * p + h) * 2 * nblk, 2 * nblk), 2 * nblk), :].reshape(cols, blk)
            for h in range(2)
        ]
        block = jnp.concatenate(halves, axis=1)
        sums = mixed_dot(lower, block, 1, 0) + mixed_dot(upper, block, 1, 0)
        first = sums.astype(jnp.bfloat16)
        second = (sums - first.astype(jnp.float32)).astype(jnp.bfloat16)
        for h in range(2):
            for odd_row in range(2):
                channel = (2 * p + h) * 2 + odd_row
                place = pl.ds(pl.multiple_of(channel * readers, readers), readers)
                for k in range(bases):
                    low_row = odd_row * codes + k * readers
                    high[place, k * blk:(k + 1) * blk] = first[low_row:low_row + readers, h * blk:(h + 1) * blk]
                    low[place, k * blk:(k + 1) * blk] = second[low_row:low_row + readers, h * blk:(h + 1) * blk]
        return carry

    lax.fori_loop(0, trip_width // 4, project, 0)

    span = 16
    for step in range(trip_width // span):
        place = slice(step * span * readers, (step + 1) * span * readers)
        total = mixed_dot(high[place, :], acat[...], 1, 1) + mixed_dot(low[place, :], acat[...], 1, 1)
        msg[step * span:(step + 1) * span] = total.reshape(span, readers, blk)
    mine = pl.ds(pl.multiple_of(r * nblk, nblk), nblk)
    other = pl.ds(pl.multiple_of((1 - r) * nblk, nblk), nblk)
    give[...] = msg[:, other, :].reshape(trip_width * nblk, blk)
    swap = pltpu.make_async_remote_copy(
        src_ref=give, dst_ref=take, send_sem=msg_send, recv_sem=msg_recv, device_id=pair, device_id_type=MESH,
    )
    swap.start()
    part[...] = msg[:, mine, :].reshape(trip_width * nblk, blk)
    swap.wait()
    part[...] = part[...] + take[...]
    for b in range(nblk):
        block = part[pl.ds(b, trip_width, stride=nblk), :].astype(jnp.bfloat16)
        trip = silu(mixed_dot(block, w_up[...], 0, 0))
        pre[b] = edges[b * blk:(b + 1) * blk, :].astype(jnp.float32) + trip

    for load in loads[2:]:
        load.wait()

    def tail(m, carry):
        bulk(m).wait_recv()
        b = jnp.int32(0)
        for j in range(nblk):
            b = jnp.where(perm[j] == m, j, b)
        span = pl.ds(pl.multiple_of(m * blk, blk), blk)
        state = ((pre[b] + mixed_dot(rev[span, :], w_rev[...], 1, 0)) * root_three).astype(jnp.bfloat16)
        for layer in range(mlp1.shape[0]):
            hidden = silu(mixed_dot(state, mlp1[layer], 1, 0)).astype(jnp.bfloat16)
            branch = silu(mixed_dot(hidden, mlp2[layer], 1, 0))
            state = ((state.astype(jnp.float32) + branch) * root_two).astype(jnp.bfloat16)
        done[m] = state
        return carry

    lax.fori_loop(0, nblk, tail, 0)

    line = lax.broadcasted_iota(jnp.int32, (blk, width), 0)
    for b in range(nblk):
        value = done[perm[b]]
        out[b * blk:(b + 1) * blk, :] = jnp.where(line + b * blk < edge_count[0], value, jnp.zeros_like(value))

    for m in range(nblk):
        bulk(m).wait_send()
    for o in range(n_src):
        chunk(o * n_rep + r, pair_send, o, pair).wait_send()

        @pl.when(jnp.logical_and(has_right, o <= s))
        def _():
            chunk(o * n_rep + r, right_send, o, right).wait_send()

        @pl.when(jnp.logical_and(has_left, o >= s))
        def _():
            chunk(o * n_rep + r, left_send, o, left).wait_send()


def solution(mesh):
    n_src, n_dst, n_rep = mesh.shape["src"], mesh.shape["dst"], mesh.shape["rep"]

    def local(edges, edge_count, triplets, trip_count, rev_perm, w_down, w_up, w_rev, w_mlp1, w_mlp2, angular):
        rows, width = edges.shape[3], edges.shape[4]
        bases, blk = angular.shape[0], angular.shape[1]
        nblk = rows // blk
        trip_width = w_down.shape[1]
        readers = n_rep * nblk
        kind, full = jnp.bfloat16, jnp.float32
        smem = pl.BlockSpec(memory_space=pltpu.SMEM)
        vmem = pl.BlockSpec(memory_space=pltpu.VMEM)
        hbm = pl.BlockSpec(memory_space=pl.ANY)
        dma = pltpu.SemaphoreType.DMA
        out = pl.pallas_call(
            functools.partial(kernel, (n_src, n_dst, n_rep)),
            out_shape=jax.ShapeDtypeStruct((rows, width), kind),
            in_specs=[smem] * 3 + [vmem] * 3 + [hbm] * 5,
            out_specs=vmem,
            scratch_shapes=[
                pltpu.VMEM((rows, width), kind),
                pltpu.VMEM((rows, width), kind),
                pltpu.VMEM(w_rev.shape, kind),
                pltpu.VMEM(w_mlp1.shape, kind),
                pltpu.VMEM(w_mlp2.shape, kind),
                pltpu.VMEM(angular.shape, kind),
                pltpu.VMEM((blk, bases * blk), kind),
                pltpu.VMEM((trip_width * nblk, blk), full),
                pltpu.VMEM((n_src * n_rep, trip_width * nblk, blk), kind),
                pltpu.VMEM((trip_width * readers, bases * blk), kind),
                pltpu.VMEM((trip_width * readers, bases * blk), kind),
                pltpu.VMEM((trip_width, readers, blk), full),
                pltpu.VMEM((trip_width * nblk, blk), full),
                pltpu.VMEM((trip_width * nblk, blk), full),
                pltpu.VMEM((trip_width * nblk, blk), full),
                pltpu.VMEM((nblk, blk, width), full),
                pltpu.VMEM((nblk, blk, width), kind),
                dma((5,)),
                dma((nblk,)),
                dma((nblk,)),
                dma((n_src,)),
                dma((n_src,)),
                dma((n_src,)),
                dma((n_src * n_rep,)),
                dma,
                dma,
            ],
            compiler_params=pltpu.CompilerParams(
                collective_id=0, has_side_effects=True, vmem_limit_bytes=48 << 20
            ),
        )(
            edge_count.reshape(1), trip_count.reshape(1), rev_perm.reshape(nblk), triplets.reshape(3, -1),
            w_down, w_up, edges.reshape(rows, width), w_rev, w_mlp1, w_mlp2, angular,
        )
        return out.reshape(1, 1, 1, rows, width)

    split = ("parts", "src"), "dst", "rep"
    in_specs = (
        P(*split, None, None),
        P(*split),
        P(*split, None, None),
        P(*split),
        P(*split, None),
    ) + (P(),) * 6
    return jax.shard_map(local, mesh=mesh, in_specs=in_specs, out_specs=P(*split, None, None), check_vma=False)
```

time: 102 us -> 94.6 us (0.927)
  the two profiles are of different devices: /device:TPU:8 before, /device:TPU:0 now
where the time goes in v2:
time: 94.6 us; the launch traced here: 94.2 us
  Pallas kernels  84.1 us (89%)
  local copies, waits for them, and re-layouts  8.83 us (9%)
  between operations  1.33 us (1%)
    pallas_call x1, Pallas kernels, local(): pl.pallas_call(functools.partial(kernel, (n_src, n_dst, n_rep)), out_shap...  84.1 us
    unnamed x15, local copies, waits for them, and re-layouts  8.83 us

profile of v2, /device:TPU:0, one launch (start us, length us, event | category | flops | bytes accessed | tf_op | source)
XLA Modules:
  0.0 94.2 jit_solution(4380929221824271636)
XLA Ops:
  1.3 0.7 copy.15
  2.0 1.0 %copy.12.w_down = bf16[512,64]{1,0:T(8,128)(2,1)S(1)} copy(bf16[512,64]{0,1:T(8,128)(2,1)} %param.16) | data formatting | bytes 131072 | tf_op args[5]
  3.0 0.0 copy-start
  3.0 1.4 %copy-done = bf16[3,512,512]{2,1,0:T(8,128)(2,1)S(1)} copy-done((bf16[3,512,512]{2,1,0:T(8,128)(2,1)S(1)}, bf16[3,512,512]{2,1,0:T(8,128)(2,1)}, u32[]{:S(2)}) %copy-start) | copy-done | bytes 1572888
  4.4 0.0 copy-start.1
  4.4 1.2 %copy-done.1 = bf16[1,1,1,1024,512]{4,3,2,1,0:T(8,128)(2,1)S(1)} copy-done((bf16[1,1,1,1024,512]{4,3,2,1,0:T(8,128)(2,1)S(1)}, bf16[1,1,1,1024,512]{4,3,2,1,0:T(8,128)(2,1)}, u32[]{:S(2)}) %copy-start.1) | copy-done | bytes 1048600
  5.6 0.0 copy-start.2
  5.6 1.0 %copy-done.2 = bf16[512,512]{1,0:T(8,128)(2,1)S(1)} copy-done((bf16[512,512]{1,0:T(8,128)(2,1)S(1)}, bf16[512,512]{1,0:T(8,128)(2,1)}, u32[]{:S(2)}) %copy-start.2) | copy-done | bytes 524312
  6.6 0.0 copy-start.3
  6.6 1.0 %copy-done.3 = bf16[16,128,128]{2,1,0:T(8,128)(2,1)S(1)} copy-done((bf16[16,128,128]{2,1,0:T(8,128)(2,1)S(1)}, bf16[16,128,128]{2,1,0:T(8,128)(2,1)}, u32[]{:S(2)}) %copy-start.3) | copy-done | bytes 524312
  7.7 0.0 copy-start.4
  7.7 0.8 copy-done.4
  8.5 0.0 copy-start.5
  8.5 0.7 copy-done.5
  9.2 84.1 %shard_map.109 = bf16[1024,512]{1,0:T(8,128)(2,1)S(1)} custom-call(s32[1]{0:T(128)} %bitcast.8.edge_count, s32[1]{0:T(128)} %bitcast.9.trip_count, s32[8]{0:T(128)S(1)} %bitcast.13, s32[3,512]{1,0:T(4,128)S(1)} %bitcast.12, bf16[512,64]{1,0:T(8,128)(2,1)S(1)} %copy.12.w_down, bf16[64,512]{1,0:T(8,128)(2,1)S(1)} %copy-done.4, bf16[1024,512]{1,0:T(8,128)(2,1)S(1)} %bitcast.11, ...), custom_call_target="tpu_custom_call" | custom-call | tf_op jit(solution)/shard_map/pallas_call | solution.py:247
  93.2 1.0 %copy.19 = bf16[1,1,1,1024,512]{4,3,2,1,0:T(8,128)(2,1)} copy(bf16[1,1,1,1024,512]{4,3,2,1,0:T(8,128)(2,1)S(1)} %bitcast.10) | data formatting | bytes 2097152
Async XLA Ops:
  3.0 1.4 %copy-start = (bf16[3,512,512]{2,1,0:T(8,128)(2,1)S(1)}, bf16[3,512,512]{2,1,0:T(8,128)(2,1)}, u32[]{:S(2)}) copy-start(bf16[3,512,512]{2,1,0:T(8,128)(2,1)} %mlp1_in.1) | copy-start | bytes 4718596
  4.4 1.2 %copy-start.1 = (bf16[1,1,1,1024,512]{4,3,2,1,0:T(8,128)(2,1)S(1)}, bf16[1,1,1,1024,512]{4,3,2,1,0:T(8,128)(2,1)}, u32[]{:S(2)}) copy-start(bf16[1,1,1,1024,512]{4,3,2,1,0:T(8,128)(2,1)} %param.11) | copy-start | bytes 3145732
  5.6 1.0 %copy-start.2 = (bf16[512,512]{1,0:T(8,128)(2,1)S(1)}, bf16[512,512]{1,0:T(8,128)(2,1)}, u32[]{:S(2)}) copy-start(bf16[512,512]{1,0:T(8,128)(2,1)} %rev_in.1) | copy-start | bytes 1572868
  6.6 1.0 %copy-start.3 = (bf16[16,128,128]{2,1,0:T(8,128)(2,1)S(1)}, bf16[16,128,128]{2,1,0:T(8,128)(2,1)}, u32[]{:S(2)}) copy-start(bf16[16,128,128]{2,1,0:T(8,128)(2,1)} %ang_in.1) | copy-start | bytes 1572868
  7.7 0.8 copy-start.4
  8.5 0.7 copy-start.5

commit v3 on v2

--- a/solution.py
+++ b/solution.py
@@ -10,7 +10,12 @@
 root_three = 3.0 ** (-0.5)
 root_two = 2.0 ** (-0.5)
 MESH = pl.DeviceIdType.MESH
-HEAD = 3
+PIECE = 64
+HEAD = 2
+GAP = 1
+MIDDLE = 4
+LATE = 2
+FAST = False
 
 
 def silu(v):
@@ -66,9 +71,10 @@
     pl.semaphore_wait(barrier, 2 + has_right.astype(jnp.int32) + has_left.astype(jnp.int32))
 
     def bulk(m):
-        span = pl.ds(pl.multiple_of(m * blk, blk), blk)
+        span = pl.ds(pl.multiple_of(m * PIECE, PIECE), PIECE)
+        source = edges if FAST else edges_in
         return pltpu.make_async_remote_copy(
-            src_ref=edges_in.at[span], dst_ref=rev.at[span],
+            src_ref=source.at[span], dst_ref=rev.at[span],
             send_sem=bulk_send.at[m], recv_sem=bulk_recv.at[m], device_id=mirror, device_id_type=MESH,
         )
 
@@ -78,10 +84,19 @@
             send_sem=sems.at[o], recv_sem=gath_recv.at[q], device_id=target, device_id_type=MESH,
         )
 
-    for m in range(HEAD):
-        bulk(m).start()
-
-    loads[0].wait()
+    pieces = rows // PIECE
+    queue = list(range(pieces))
+
+    def send(count):
+        for m in queue[:count]:
+            bulk(m).start()
+        del queue[:count]
+
+    if FAST:
+        loads[0].wait()
+    send(HEAD)
+    if not FAST:
+        loads[0].wait()
     lane = lax.broadcasted_iota(jnp.int32, (trip_width, blk), 1)
     down = w_down[...]
     for b in range(nblk):
@@ -100,9 +115,7 @@
     def _():
         chunk(own, left_send, s, left).start()
 
-    for m in range(HEAD, nblk):
-        bulk(m).start()
-
+    send(GAP)
     loads[1].wait()
     for k in range(bases):
         acat[:, k * blk:(k + 1) * blk] = ang[k]
@@ -148,6 +161,10 @@
 
             chunk(q, pair_send, o, pair).start()
 
+        if hop < n_src - 1:
+            send(GAP)
+
+    send(MIDDLE)
     for o in range(n_src):
         chunk(o * n_rep + 1 - r, pair_send, o, pair).wait_recv()
 
@@ -171,6 +188,7 @@
         return carry
 
     lax.fori_loop(0, trip_width // 4, project, 0)
+    send(LATE)
 
     span = 16
     for step in range(trip_width // span):
@@ -184,6 +202,7 @@
         src_ref=give, dst_ref=take, send_sem=msg_send, recv_sem=msg_recv, device_id=pair, device_id_type=MESH,
     )
     swap.start()
+    send(len(queue))
     part[...] = msg[:, mine, :].reshape(trip_width * nblk, blk)
     swap.wait()
     part[...] = part[...] + take[...]
@@ -196,7 +215,8 @@
         load.wait()
 
     def tail(m, carry):
-        bulk(m).wait_recv()
+        for j in range(blk // PIECE):
+            bulk(m * (blk // PIECE) + j).wait_recv()
         b = jnp.int32(0)
         for j in range(nblk):
             b = jnp.where(perm[j] == m, j, b)
@@ -216,7 +236,7 @@
         value = done[perm[b]]
         out[b * blk:(b + 1) * blk, :] = jnp.where(line + b * blk < edge_count[0], value, jnp.zeros_like(value))
 
-    for m in range(nblk):
+    for m in range(pieces):
         bulk(m).wait_send()
     for o in range(n_src):
         chunk(o * n_rep + r, pair_send, o, pair).wait_send()
@@ -268,8 +288,8 @@
                 pltpu.VMEM((nblk, blk, width), full),
                 pltpu.VMEM((nblk, blk, width), kind),
                 dma((5,)),
-                dma((nblk,)),
-                dma((nblk,)),
+                dma((rows // PIECE,)),
+                dma((rows // PIECE,)),
                 dma((n_src,)),
                 dma((n_src,)),
                 dma((n_src,)),

time: 94.6 us -> 68.7 us (0.73)
  the two profiles are of different devices: /device:TPU:0 before, /device:TPU:8 now
where the time goes in v3:
time: 68.7 us; the launch traced here: 68.3 us
  Pallas kernels  58.1 us (85%)
  local copies, waits for them, and re-layouts  8.83 us (13%)
  between operations  1.33 us (2%)
    pallas_call x1, Pallas kernels, local(): pl.pallas_call(functools.partial(kernel, (n_src, n_dst, n_rep)), out_shap...  58.1 us
    unnamed x15, local copies, waits for them, and re-layouts  8.83 us

profile of v3, /device:TPU:8, one launch (start us, length us, event | category | flops | bytes accessed | tf_op | source)
XLA Modules:
  0.0 68.3 jit_solution(7993982985757595785)
XLA Ops:
  1.3 0.7 %copy.15 = s32[1,1,1,3,512]{4,3,2,1,0:T(4,128)S(1)} copy(s32[1,1,1,3,512]{4,2,3,1,0:T(1,128)} %param.13) | data formatting | bytes 12288
  2.0 1.0 %copy.12.w_down = bf16[512,64]{1,0:T(8,128)(2,1)S(1)} copy(bf16[512,64]{0,1:T(8,128)(2,1)} %param.16) | data formatting | bytes 131072 | tf_op args[5]
  3.0 0.0 copy-start
  3.0 1.4 %copy-done = bf16[3,512,512]{2,1,0:T(8,128)(2,1)S(1)} copy-done((bf16[3,512,512]{2,1,0:T(8,128)(2,1)S(1)}, bf16[3,512,512]{2,1,0:T(8,128)(2,1)}, u32[]{:S(2)}) %copy-start) | copy-done | bytes 1572888
  4.4 0.0 copy-start.1
  4.4 1.2 %copy-done.1 = bf16[1,1,1,1024,512]{4,3,2,1,0:T(8,128)(2,1)S(1)} copy-done((bf16[1,1,1,1024,512]{4,3,2,1,0:T(8,128)(2,1)S(1)}, bf16[1,1,1,1024,512]{4,3,2,1,0:T(8,128)(2,1)}, u32[]{:S(2)}) %copy-start.1) | copy-done | bytes 1048600
  5.6 0.0 copy-start.2
  5.6 1.0 %copy-done.2 = bf16[512,512]{1,0:T(8,128)(2,1)S(1)} copy-done((bf16[512,512]{1,0:T(8,128)(2,1)S(1)}, bf16[512,512]{1,0:T(8,128)(2,1)}, u32[]{:S(2)}) %copy-start.2) | copy-done | bytes 524312
  6.6 0.0 copy-start.3
  6.6 1.0 %copy-done.3 = bf16[16,128,128]{2,1,0:T(8,128)(2,1)S(1)} copy-done((bf16[16,128,128]{2,1,0:T(8,128)(2,1)S(1)}, bf16[16,128,128]{2,1,0:T(8,128)(2,1)}, u32[]{:S(2)}) %copy-start.3) | copy-done | bytes 524312
  7.7 0.0 copy-start.4
  7.7 0.8 %copy-done.4 = bf16[64,512]{1,0:T(8,128)(2,1)S(1)} copy-done((bf16[64,512]{1,0:T(8,128)(2,1)S(1)}, bf16[64,512]{1,0:T(8,128)(2,1)}, u32[]{:S(2)}) %copy-start.4) | copy-done | bytes 65560
  8.5 0.0 copy-start.5
  8.5 0.7 copy-done.5
  9.2 58.1 %shard_map.109 = bf16[1024,512]{1,0:T(8,128)(2,1)S(1)} custom-call(s32[1]{0:T(128)} %bitcast.8.edge_count, s32[1]{0:T(128)} %bitcast.9.trip_count, s32[8]{0:T(128)S(1)} %bitcast.13, s32[3,512]{1,0:T(4,128)S(1)} %bitcast.12, bf16[512,64]{1,0:T(8,128)(2,1)S(1)} %copy.12.w_down, bf16[64,512]{1,0:T(8,128)(2,1)S(1)} %copy-done.4, bf16[1024,512]{1,0:T(8,128)(2,1)S(1)} %bitcast.11, ...), custom_call_target="tpu_custom_call" | custom-call | tf_op jit(solution)/shard_map/pallas_call | solution.py:267
  67.3 1.0 %copy.19 = bf16[1,1,1,1024,512]{4,3,2,1,0:T(8,128)(2,1)} copy(bf16[1,1,1,1024,512]{4,3,2,1,0:T(8,128)(2,1)S(1)} %bitcast.10) | data formatting | bytes 2097152
Async XLA Ops:
  3.0 1.4 %copy-start = (bf16[3,512,512]{2,1,0:T(8,128)(2,1)S(1)}, bf16[3,512,512]{2,1,0:T(8,128)(2,1)}, u32[]{:S(2)}) copy-start(bf16[3,512,512]{2,1,0:T(8,128)(2,1)} %mlp1_in.1) | copy-start | bytes 4718596
  4.4 1.2 %copy-start.1 = (bf16[1,1,1,1024,512]{4,3,2,1,0:T(8,128)(2,1)S(1)}, bf16[1,1,1,1024,512]{4,3,2,1,0:T(8,128)(2,1)}, u32[]{:S(2)}) copy-start(bf16[1,1,1,1024,512]{4,3,2,1,0:T(8,128)(2,1)} %param.11) | copy-start | bytes 3145732
  5.6 1.0 %copy-start.2 = (bf16[512,512]{1,0:T(8,128)(2,1)S(1)}, bf16[512,512]{1,0:T(8,128)(2,1)}, u32[]{:S(2)}) copy-start(bf16[512,512]{1,0:T(8,128)(2,1)} %rev_in.1) | copy-start | bytes 1572868
  6.6 1.0 %copy-start.3 = (bf16[16,128,128]{2,1,0:T(8,128)(2,1)S(1)}, bf16[16,128,128]{2,1,0:T(8,128)(2,1)}, u32[]{:S(2)}) copy-start(bf16[16,128,128]{2,1,0:T(8,128)(2,1)} %ang_in.1) | copy-start | bytes 1572868
  7.7 0.8 %copy-start.4 = (bf16[64,512]{1,0:T(8,128)(2,1)S(1)}, bf16[64,512]{1,0:T(8,128)(2,1)}, u32[]{:S(2)}) copy-start(bf16[64,512]{1,0:T(8,128)(2,1)} %w_up.1) | copy-start | bytes 196612
  8.5 0.7 copy-start.5

commit v4 on v3

--- a/solution.py
+++ b/solution.py
@@ -27,8 +27,8 @@
 
 
 def kernel(
-    sizes, edge_count, trip_count, perm, lists, w_down, w_up, edges_in, rev_in, mlp1_in, mlp2_in, ang_in, out,
-    edges, rev, w_rev, mlp1, mlp2, ang, acat, proj, gath, high, low, msg, part, give, take, pre, done,
+    sizes, edge_count, trip_count, perm, lists_in, down_in, up_in, edges_in, rev_in, mlp1_in, mlp2_in, ang_in, out,
+    lists, w_down, w_up, edges, rev, w_rev, mlp1, mlp2, ang, acat, proj, gath, high, low, msg, part, give, take, pre, done,
     load_sem, bulk_send, bulk_recv, right_send, left_send, pair_send, gath_recv, msg_send, msg_recv,
 ):
     n_src, n_dst, n_rep = sizes
@@ -37,8 +37,8 @@
     bases, blk = ang.shape[0], ang.shape[1]
     nblk = rows // blk
     shift = nblk.bit_length() - 1
-    trip_width = w_down.shape[1]
-    slots = lists.shape[1]
+    trip_width = w_down.shape[0]
+    slots = lists.shape[2]
     readers = n_rep * nblk
     codes = readers * bases
     mirror = {"src": n_src - 1 - s, "dst": n_dst - 1 - d}
@@ -50,7 +50,10 @@
     loads = [
         pltpu.make_async_copy(source, target, load_sem.at[index])
         for index, (source, target) in enumerate(
-            [(edges_in, edges), (ang_in, ang), (rev_in, w_rev), (mlp1_in, mlp1), (mlp2_in, mlp2)]
+            [
+                (edges_in, edges), (down_in, w_down), (lists_in, lists), (ang_in, ang),
+                (up_in, w_up), (rev_in, w_rev), (mlp1_in, mlp1), (mlp2_in, mlp2),
+            ]
         )
     ]
     for load in loads:
@@ -97,11 +100,12 @@
     send(HEAD)
     if not FAST:
         loads[0].wait()
+    loads[1].wait()
     lane = lax.broadcasted_iota(jnp.int32, (trip_width, blk), 1)
     down = w_down[...]
     for b in range(nblk):
-        value = silu(mixed_dot(down, edges[b * blk:(b + 1) * blk, :], 0, 1))
-        value = jnp.where(lane + b * blk < edge_count[0], value, 0.0)
+        value = silu(mixed_dot(down, edges[b * blk:(b + 1) * blk, :], 1, 1))
+        value = jnp.where(lane + b * blk < edge_count[0, 0, 0], value, 0.0)
         proj[pl.ds(b, trip_width, stride=nblk), :] = value
     own = s * n_rep + r
     gath[own] = proj[...].astype(jnp.bfloat16)
@@ -116,12 +120,13 @@
         chunk(own, left_send, s, left).start()
 
     send(GAP)
-    loads[1].wait()
+    loads[2].wait()
+    loads[3].wait()
     for k in range(bases):
         acat[:, k * blk:(k + 1) * blk] = ang[k]
-    a, c, k = lists[0:1, :], lists[1:2, :], lists[2:3, :]
+    a, c, k = lists[0], lists[1], lists[2]
     slot = lax.broadcasted_iota(jnp.int32, (1, slots), 1)
-    code = jnp.where(slot < trip_count[0], k * readers + a, -1)
+    code = jnp.where(slot < trip_count[0, 0, 0], k * readers + a, -1)
     hot_code = jnp.where(lax.broadcasted_iota(jnp.int32, (codes, slots), 0) == code, 1.0, 0.0).astype(jnp.bfloat16)
     cols = n_src * n_rep * nblk * 2
     line = lax.broadcasted_iota(jnp.int32, (cols, slots), 0)
@@ -206,12 +211,13 @@
     part[...] = msg[:, mine, :].reshape(trip_width * nblk, blk)
     swap.wait()
     part[...] = part[...] + take[...]
+    loads[4].wait()
     for b in range(nblk):
         block = part[pl.ds(b, trip_width, stride=nblk), :].astype(jnp.bfloat16)
         trip = silu(mixed_dot(block, w_up[...], 0, 0))
         pre[b] = edges[b * blk:(b + 1) * blk, :].astype(jnp.float32) + trip
 
-    for load in loads[2:]:
+    for load in loads[5:]:
         load.wait()
 
     def tail(m, carry):
@@ -219,7 +225,7 @@
             bulk(m * (blk // PIECE) + j).wait_recv()
         b = jnp.int32(0)
         for j in range(nblk):
-            b = jnp.where(perm[j] == m, j, b)
+            b = jnp.where(perm[0, 0, 0, j] == m, j, b)
         span = pl.ds(pl.multiple_of(m * blk, blk), blk)
         state = ((pre[b] + mixed_dot(rev[span, :], w_rev[...], 1, 0)) * root_three).astype(jnp.bfloat16)
         for layer in range(mlp1.shape[0]):
@@ -233,8 +239,8 @@
 
     line = lax.broadcasted_iota(jnp.int32, (blk, width), 0)
     for b in range(nblk):
-        value = done[perm[b]]
-        out[b * blk:(b + 1) * blk, :] = jnp.where(line + b * blk < edge_count[0], value, jnp.zeros_like(value))
+        value = done[perm[0, 0, 0, b]]
+        out[b * blk:(b + 1) * blk, :] = jnp.where(line + b * blk < edge_count[0, 0, 0], value, jnp.zeros_like(value))
 
     for m in range(pieces):
         bulk(m).wait_send()
@@ -262,14 +268,17 @@
         kind, full = jnp.bfloat16, jnp.float32
         smem = pl.BlockSpec(memory_space=pltpu.SMEM)
         vmem = pl.BlockSpec(memory_space=pltpu.VMEM)
-        hbm = pl.BlockSpec(memory_space=pl.ANY)
+        hbm = pl.BlockSpec(memory_space=pltpu.HBM)
         dma = pltpu.SemaphoreType.DMA
         out = pl.pallas_call(
             functools.partial(kernel, (n_src, n_dst, n_rep)),
             out_shape=jax.ShapeDtypeStruct((rows, width), kind),
-            in_specs=[smem] * 3 + [vmem] * 3 + [hbm] * 5,
+            in_specs=[smem] * 3 + [hbm] * 8,
             out_specs=vmem,
             scratch_shapes=[
+                pltpu.VMEM((3, 1, triplets.shape[4]), jnp.int32),
+                pltpu.VMEM((trip_width, width), kind),
+                pltpu.VMEM(w_up.shape, kind),
                 pltpu.VMEM((rows, width), kind),
                 pltpu.VMEM((rows, width), kind),
                 pltpu.VMEM(w_rev.shape, kind),
@@ -287,7 +296,7 @@
                 pltpu.VMEM((trip_width * nblk, blk), full),
                 pltpu.VMEM((nblk, blk, width), full),
                 pltpu.VMEM((nblk, blk, width), kind),
-                dma((5,)),
+                dma((8,)),
                 dma((rows // PIECE,)),
                 dma((rows // PIECE,)),
                 dma((n_src,)),
@@ -298,11 +307,11 @@
                 dma,
             ],
             compiler_params=pltpu.CompilerParams(
-                collective_id=0, has_side_effects=True, vmem_limit_bytes=48 << 20
+                collective_id=0, has_side_effects=True, vmem_limit_bytes=60 << 20
             ),
         )(
-            edge_count.reshape(1), trip_count.reshape(1), rev_perm.reshape(nblk), triplets.reshape(3, -1),
-            w_down, w_up, edges.reshape(rows, width), w_rev, w_mlp1, w_mlp2, angular,
+            edge_count, trip_count, rev_perm, triplets.reshape(3, 1, -1),
+            w_down.T, w_up, edges.reshape(rows, width), w_rev, w_mlp1, w_mlp2, angular,
         )
         return out.reshape(1, 1, 1, rows, width)
 

time: 68.7 us -> 63 us (0.917)
  local copies, waits for them, and re-layouts: 8.83 us -> 2.26 us
  Pallas kernels: 58.1 us -> 59.2 us
    unnamed x15 -> x1, local copies, waits for them, and re-layouts: 8.83 us -> 2.26 us
    pallas_call x1, Pallas kernels: 58.1 us -> 59.2 us  [local(): pl.pallas_call(functools.partial(kernel, (n_src, n_dst, n_rep)), out_shap...]
where the time goes in v4:
time: 63 us; the launch traced here: 62.8 us
  Pallas kernels  59.2 us (94%)
  local copies, waits for them, and re-layouts  2.26 us (4%)
  between operations  1.3 us (2%)
    pallas_call x1, Pallas kernels, local(): pl.pallas_call(functools.partial(kernel, (n_src, n_dst, n_rep)), out_shap...  59.2 us
    unnamed x1, local copies, waits for them, and re-layouts  2.26 us

profile of v4, /device:TPU:8, one launch (start us, length us, event | category | flops | bytes accessed | tf_op | source)
XLA Modules:
  0.0 62.8 jit_solution(17289621936509541132)
XLA Ops:
  1.3 59.2 %shard_map.109 = bf16[1024,512]{1,0:T(8,128)(2,1)} custom-call(s32[1,1,1]{2,1,0:T(1,128)S(6)} %copy.13.edge_count, s32[1,1,1]{2,1,0:T(1,128)S(6)} %copy.14.trip_count, s32[1,1,1,8]{3,2,1,0:T(1,128)} %perm.1, s32[3,1,512]{2,1,0:T(1,128)} %bitcast.7, bf16[64,512]{1,0:T(8,128)(2,1)} %bitcast.6, bf16[64,512]{1,0:T(8,128)(2,1)} %up_in.1, ...), custom_call_target="tpu_custom_call" | custom-call | tf_op jit(solution)/shard_map/pallas_call | solution.py:273
  60.6 2.3 %copy.15 = bf16[1,1,1,1024,512]{4,3,2,1,0:T(8,128)(2,1)} copy(bf16[1,1,1,1024,512]{4,3,2,1,0:T(8,128)(2,1)} %bitcast.4) | data formatting | bytes 2097152

commit v5 on v4

--- a/solution.py
+++ b/solution.py
@@ -226,13 +226,20 @@
         b = jnp.int32(0)
         for j in range(nblk):
             b = jnp.where(perm[0, 0, 0, j] == m, j, b)
-        span = pl.ds(pl.multiple_of(m * blk, blk), blk)
-        state = ((pre[b] + mixed_dot(rev[span, :], w_rev[...], 1, 0)) * root_three).astype(jnp.bfloat16)
+        half = blk // 2
+        states = []
+        for side in range(2):
+            span = pl.ds(pl.multiple_of(m * blk + side * half, half), half)
+            mixed = pre[b, side * half:(side + 1) * half] + mixed_dot(rev[span, :], w_rev[...], 1, 0)
+            states.append((mixed * root_three).astype(jnp.bfloat16))
         for layer in range(mlp1.shape[0]):
-            hidden = silu(mixed_dot(state, mlp1[layer], 1, 0)).astype(jnp.bfloat16)
-            branch = silu(mixed_dot(hidden, mlp2[layer], 1, 0))
-            state = ((state.astype(jnp.float32) + branch) * root_two).astype(jnp.bfloat16)
-        done[m] = state
+            hidden = [silu(mixed_dot(state, mlp1[layer], 1, 0)).astype(jnp.bfloat16) for state in states]
+            branches = [silu(mixed_dot(value, mlp2[layer], 1, 0)) for value in hidden]
+            states = [
+                ((state.astype(jnp.float32) + branch) * root_two).astype(jnp.bfloat16)
+                for state, branch in zip(states, branches)
+            ]
+        done[m] = jnp.concatenate(states, axis=0)
         return carry
 
     lax.fori_loop(0, nblk, tail, 0)

time: 63 us -> 63 us (level)
  no operation moved by 1% of the time
where the time goes in v5:
time: 63 us; the launch traced here: 62.8 us
  Pallas kernels  59.3 us (94%)
  local copies, waits for them, and re-layouts  2.26 us (4%)
  between operations  1.3 us (2%)
    pallas_call x1, Pallas kernels, local(): pl.pallas_call(functools.partial(kernel, (n_src, n_dst, n_rep)), out_shap...  59.3 us
    unnamed x1, local copies, waits for them, and re-layouts  2.26 us

profile of v5, /device:TPU:8, one launch (start us, length us, event | category | flops | bytes accessed | tf_op | source)
XLA Modules:
  0.0 62.8 jit_solution(8803088111657867300)
XLA Ops:
  1.3 59.3 %shard_map.109 = bf16[1024,512]{1,0:T(8,128)(2,1)} custom-call(s32[1,1,1]{2,1,0:T(1,128)S(6)} %copy.13.edge_count, s32[1,1,1]{2,1,0:T(1,128)S(6)} %copy.14.trip_count, s32[1,1,1,8]{3,2,1,0:T(1,128)} %perm.1, s32[3,1,512]{2,1,0:T(1,128)} %bitcast.7, bf16[64,512]{1,0:T(8,128)(2,1)} %bitcast.6, bf16[64,512]{1,0:T(8,128)(2,1)} %up_in.1, ...), custom_call_target="tpu_custom_call" | custom-call | tf_op jit(solution)/shard_map/pallas_call | solution.py:280
  60.6 2.3 %copy.15 = bf16[1,1,1,1024,512]{4,3,2,1,0:T(8,128)(2,1)} copy(bf16[1,1,1,1024,512]{4,3,2,1,0:T(8,128)(2,1)} %bitcast.4) | data formatting | bytes 2097152
